TPU v7x, 32 devices: a whole 2x2x4 slice. The times are simulated.
32 devices in a mesh: row: 8 (over z, x), col: 4 (over y, core).
Axes of the slice: x: 2, y: 2, z: 4, core: 2. Of those that a mesh axis runs over, the one named last changes fastest.
Arguments:
- tile_u: bfloat16 [16, 8, 1024, 128], P('row', 'col'), may hold values from -6 to 6
- tile_v: bfloat16 [16, 8, 128, 1024], P('row', 'col'), may hold values from -0.5 to 0.5
- tile_ranks: int32 [16, 8], P('row', 'col'), may hold values from 32 to 128
- inverses: bfloat16 [2, 1024, 1024], replicated, may hold values from -0.005859375 to 0.005859375
- panel_order: int32 [2, 2], replicated, may hold values from 0 to 15, as said below
Outputs:
- trailing: bfloat16 [16, 8, 1024, 1024], P('row', 'col')
Inputs may be any that keep to these rules, and one draw needn't show every extreme that they name: `panel_order`: column 0 names 2 different tile rows, below 16; column 1 names 2 different tile columns, below 8; the last tile row and the last tile column are always among them.
All inputs are finite; a program needn't handle non-finite values.
Results may differ from a plain program's by a relative error of at most 0.0075.
Values may be sent and summed in bfloat16 or wider, within the bound.
No kernel may reach another device: no remote copies, remote signals or barrier semaphores. Data moves between devices by JAX's collectives and lax.ppermute only.
A program may use at most 128 MiB of HBM per device.

v0:
```python
import jax
import jax.numpy as jnp
from jax import lax
from jax.sharding import PartitionSpec as P

STEPS = 2


def from_root(value, axis, root):
    mine = lax.axis_index(axis) == root
    return lax.psum(jnp.where(mine, value, jnp.zeros_like(value)), axis)


def apply_inverse(inverse, pivot_left):
    return jnp.einsum(
        "bd,cdk->cbk", inverse, pivot_left, preferred_element_type=jnp.float32
    ).astype(jnp.bfloat16)


def eliminate(left_factors, right_factors, inverse, pivot_row, pivot_column, update_mask):
    rows_here = left_factors.shape[0]
    columns_here = left_factors.shape[1]
    local_row = pivot_row % rows_here
    local_column = pivot_column % columns_here
    column_left = lax.dynamic_index_in_dim(left_factors, local_column, 1, keepdims=False)
    column_right = lax.dynamic_index_in_dim(right_factors, local_column, 1, keepdims=False)
    pivot_left = lax.dynamic_index_in_dim(left_factors, local_row, 0, keepdims=False)
    pivot_right = lax.dynamic_index_in_dim(right_factors, local_row, 0, keepdims=False)
    row_root = pivot_row // rows_here
    column_root = pivot_column // columns_here
    column_left, column_right = (
        from_root(column_left, "col", column_root),
        from_root(column_right, "col", column_root),
    )
    pivot_left, pivot_right = (
        from_root(pivot_left, "row", row_root),
        from_root(pivot_right, "row", row_root),
    )
    solved = apply_inverse(inverse, pivot_left)
    core_block = jnp.einsum(
        "rkb,cbs->rcks", column_right, solved, preferred_element_type=jnp.float32
    )
    core_block = core_block.astype(jnp.bfloat16)
    update = jnp.einsum(
        "rcks,csb->rckb", core_block, pivot_right, preferred_element_type=jnp.float32
    )
    update = (update * (-update_mask)[:, :, None, None]).astype(jnp.bfloat16)
    spread = jnp.broadcast_to(
        column_left[:, None], (rows_here, columns_here) + column_left.shape[1:]
    )
    widened_left = jnp.concatenate([left_factors, spread], axis=3)
    widened_right = jnp.concatenate([right_factors, update], axis=2)
    return (widened_left, widened_right, column_left, update)


def advance(carry, inverse, pivot_row, pivot_column, row_global, column_global):
    left_factors, right_factors, row_done, column_done = carry
    row_done = jnp.logical_or(row_done, row_global == pivot_row)
    column_done = jnp.logical_or(column_done, column_global == pivot_column)
    update_mask = jnp.logical_and(
        jnp.logical_not(row_done)[:, None], jnp.logical_not(column_done)[None, :]
    ).astype(jnp.float32)
    left_factors, right_factors, column_left, update = eliminate(
        left_factors, right_factors, inverse, pivot_row, pivot_column, update_mask
    )
    return ((left_factors, right_factors, row_done, column_done), column_left, update)


def on_device(tile_u, tile_v, tile_ranks, inverses, panel_order):
    rows_here = tile_u.shape[0]
    columns_here = tile_u.shape[1]
    row_global = lax.axis_index("row") * rows_here + jnp.arange(rows_here, dtype=jnp.int32)
    column_global = lax.axis_index("col") * columns_here + jnp.arange(columns_here, dtype=jnp.int32)
    kept_rows = (
        jnp.arange(tile_v.shape[2], dtype=jnp.int32)[None, None, :] < tile_ranks[:, :, None]
    ).astype(tile_v.dtype)
    carry = (
        tile_u,
        tile_v * kept_rows[..., None],
        jnp.zeros((rows_here,), dtype=jnp.bool_),
        jnp.zeros((columns_here,), dtype=jnp.bool_),
    )
    carry, column_left, update = advance(
        carry, inverses[0], panel_order[0, 0], panel_order[0, 1], row_global, column_global
    )
    final_index = STEPS - 1
    carry, column_left, update = advance(
        carry,
        inverses[final_index],
        panel_order[final_index, 0],
        panel_order[final_index, 1],
        row_global,
        column_global,
    )
    trailing = jnp.einsum("rcbk,rckd->rcbd", carry[0], carry[1], preferred_element_type=jnp.float32)
    return trailing.astype(jnp.bfloat16)


def solution(mesh):
    placed = (P("row", "col", None, None), P("row", "col", None, None), P("row", "col"), P(), P())
    return jax.shard_map(
        on_device,
        mesh=mesh,
        in_specs=placed,
        out_specs=P("row", "col", None, None),
        check_vma=False,
    )
```

profile of v0, /device:TPU:0, one launch (start us, length us, event | category | flops | bytes accessed | tf_op | source)
XLA Modules:
  0.0 328.3 jit_solution(14072655011720800447)
XLA Ops:
  6.5 1.4 fusion.56
  11.2 1.4 broadcast_multiply_fusion
  13.4 0.8 select_bitcast_fusion
  16.6 0.8 select_bitcast_fusion.1
  17.4 0.9 select_bitcast_fusion.2
  20.6 1.2 compare_not_fusion
  21.9 31.4 %all-reduce.15.cloned.1.call-done = (bf16[2,1024,128]{2,1,0:T(8,128)(2,1)}, bf16[2,128,1024]{2,1,0:T(8,128)(2,1)}) async-done(((bf16[2,1024,128]{2,1,0:T(8,128)(2,1)}, bf16[2,128,1024]{2,1,0:T(8,128)(2,1)}), (bf16[2,1024,128]{2,1,0:T(8,128)(2,1)}, bf16[2,128,1024]{2,1,0:T(8,128)(2,1)})) %all-reduce.15.cloned.1.call-update) | async-done | bytes 1048592 | tf_op jit(solution)/shard_map/psum | solution.py:11
  53.3 1.2 broadcast_in_dim.4
  54.5 1.2 fusion.44
  55.7 80.5 %all-reduce.11.cloned.1.call-done = (bf16[2,128,1024]{2,1,0:T(8,128)(2,1)}, bf16[2,1024,128]{2,1,0:T(8,128)(2,1)}) async-done(((bf16[2,128,1024]{2,1,0:T(8,128)(2,1)}, bf16[2,1024,128]{2,1,0:T(8,128)(2,1)}), (bf16[2,128,1024]{2,1,0:T(8,128)(2,1)}, bf16[2,1024,128]{2,1,0:T(8,128)(2,1)})) %all-reduce.11.cloned.1.call-update) | async-done | bytes 1048592 | tf_op jit(solution)/shard_map/psum | solution.py:11
  136.1 2.9 fusion.30
  139.0 1.5 fusion.13
  140.5 1.0 copy-done.1
  141.4 1.2 fusion.35
  145.2 1.2 fusion.41
  146.6 1.2 fusion.38
  147.9 2.4 or_not_fusion
  150.3 43.5 %all-reduce.13.cloned.1.call-done = (bf16[2,1024,256]{2,1,0:T(8,128)(2,1)}, bf16[2,256,1024]{2,1,0:T(8,128)(2,1)}) async-done(((bf16[2,1024,256]{2,1,0:T(8,128)(2,1)}, bf16[2,256,1024]{2,1,0:T(8,128)(2,1)}), (bf16[2,1024,256]{2,1,0:T(8,128)(2,1)}, bf16[2,256,1024]{2,1,0:T(8,128)(2,1)})) %all-reduce.13.cloned.1.call-update) | async-done | bytes 2097168 | tf_op jit(solution)/shard_map/psum | solution.py:11
  193.8 106.3 %all-reduce.9.cloned.1.call-done = (bf16[2,256,1024]{2,1,0:T(8,128)(2,1)}, bf16[2,1024,256]{2,1,0:T(8,128)(2,1)}) async-done(((bf16[2,256,1024]{2,1,0:T(8,128)(2,1)}, bf16[2,1024,256]{2,1,0:T(8,128)(2,1)}), (bf16[2,256,1024]{2,1,0:T(8,128)(2,1)}, bf16[2,1024,256]{2,1,0:T(8,128)(2,1)})) %all-reduce.9.cloned.1.call-update) | async-done | bytes 2097168 | tf_op jit(solution)/shard_map/psum | solution.py:11
  300.1 4.8 %convolution_convert_fusion.1 = bf16[2,256,2,256]{3,1,2,0:T(8,128)(2,1)} fusion(bf16[2,256,1024]{2,1,0:T(8,128)(2,1)} %get-tuple-element.10, bf16[2,1024,256]{2,1,0:T(8,128)(2,1)} %get-tuple-element.6, bf16[2,1024,1024]{2,1,0:T(8,128)(2,1)} %param.8), kind=kOutput, calls=%fused_computation.32 | convolution fusion | flops 1611399168 | bytes 4718592 | tf_op jit(solution)/shard_map/rkb,cbs->rcks/dot_general | solution.py:40
  304.9 1.6 copy.19
  306.4 3.4 %fusion.10 = bf16[2,2,256,1024]{3,2,1,0:T(8,128)(2,1)} fusion(f32[2,2]{1,0:T(2,128)S(1)} %fusion.54, bf16[2,256,1024]{2,1,0:T(8,128)(2,1)} %get-tuple-element.5, bf16[2,2,256,256]{2,0,3,1:T(2,128)(2,1)S(1)} %bitcast.83), kind=kOutput, calls=%fused_computation.12 | convolution fusion | flops 538968064 | bytes 3670032 | tf_op jit(solution)/shard_map/rcks,csb->rckb/dot_general | solution.py:44
  309.9 1.5 broadcast_in_dim.5
  311.3 10.4 %convolution_convert_fusion = bf16[2,2,1024,1024]{3,2,1,0:T(8,128)(2,1)} fusion(bf16[2,2,1024,256]{3,2,1,0:T(8,128)(2,1)} %broadcast_in_dim.5, bf16[2,2,1024,128]{3,2,1,0:T(8,128)(2,1)S(1)} %broadcast_in_dim.4, bf16[2,2,1024,128]{3,2,1,0:T(8,128)(2,1)S(1)} %copy-done, bf16[2,2,256,1024]{3,2,1,0:T(8,128)(2,1)} %fusion.10, ...), kind=kOutput, calls=%fused_computation | convolution fusion | flops 4324327424 | bytes 16777216 | tf_op jit(solution)/shard_map/rcbk,rckd->rcbd/dot_general | solution.py:95
  (19 shorter events, 2.1 us)
Async XLA Ops:
  6.5 6.0 %copy-start = (bf16[2,2,1024,128]{3,2,1,0:T(8,128)(2,1)S(1)}, bf16[2,2,1024,128]{3,2,1,0:T(8,128)(2,1)}, u32[]{:S(2)}) copy-start(bf16[2,2,1024,128]{3,2,1,0:T(8,128)(2,1)} %param.5) | copy-start | bytes 3145732
  6.5 46.7 %all-reduce.15.cloned.1.call-start = ((), (), s32[]{:S(2)}) async-start(), calls=%async_computation.3 | async-start | bytes 2097152 | tf_op jit(solution)/shard_map/psum | solution.py:11
  14.3 121.8 %all-reduce.11.cloned.1.call-start = ((), (), s32[]{:S(2)}) async-start(), calls=%async_computation.1 | async-start | bytes 2097152 | tf_op jit(solution)/shard_map/psum | solution.py:11
  18.3 175.5 %all-reduce.13.cloned.1.call-start = ((), (), s32[]{:S(2)}) async-start(), calls=%async_computation.2 | async-start | bytes 4194304 | tf_op jit(solution)/shard_map/psum | solution.py:11
  140.5 1.0 copy-start.1
  142.7 157.4 %all-reduce.9.cloned.1.call-start = ((), (), s32[]{:S(2)}) async-start(), calls=%async_computation | async-start | bytes 4194304 | tf_op jit(solution)/shard_map/psum | solution.py:11
  145.2 1.4 copy-start.2
  306.4 3.4 %copy-start.3 = (bf16[2,1024,256]{2,1,0:T(8,128)(2,1)S(1)}, bf16[2,1024,256]{2,1,0:T(8,128)(2,1)}, u32[]{:S(2)}) copy-start(bf16[2,1024,256]{2,1,0:T(8,128)(2,1)} %get-tuple-element.9) | copy-start | bytes 3145732
Sparse Core Ops, SparseCore 0:
  14.4 38.8 all-reduce.14
  57.2 78.8 all-reduce.10
  142.8 50.9 all-reduce.12
  197.8 102.2 all-reduce.8
where the time goes:
time: 329 us; the launch traced here: 328 us
  waiting for transfers between devices  262 us (80%)
  matrix products  23 us (7%)
  between operations  22.7 us (7%)
  other arithmetic  14 us (4%)
  local copies, waits for them, and re-layouts  6.75 us (2%)
    psum x4, waiting for transfers between devices, from_root(): return lax.psum(jnp.where(mine, value, jnp.zeros_like(value)), axis)  262 us
    dot_general x1, matrix products, on_device(): jnp.einsum('rcbk,rckd->rcbd', carry[0], carry[1], preferred_element_type=...  10.4 us
    select_n x8, other arithmetic, from_root(): return lax.psum(jnp.where(mine, value, jnp.zeros_like(value)), axis)  8.24 us
    dot_general x2, matrix products, eliminate(): jnp.einsum('rkb,cbs->rcks', column_right, solved, preferred_element_type=...  7.69 us
  transfers between devices with their start and end apart: 4, of which 4 were waited for; matrix products, arithmetic and copies ran while one was open for 3% of the time, Pallas kernels for 0%

commit v1 on v0

v1 whole, which is shorter than its diff:
```python
import jax
import jax.numpy as jnp
from jax import lax
from jax.sharding import PartitionSpec as P

F32 = jnp.float32
BF16 = jnp.bfloat16


def pick(array, index, axis=0):
    return lax.dynamic_index_in_dim(array, index, axis, keepdims=False)


def spread(parts, axis, n, root):
    me = lax.axis_index(axis)
    side = me % 2
    known = isinstance(root, int)
    bits = [1 << b for b in range(1, n.bit_length() - 1)]
    if known:
        bits = bits[::-1]
    holders = {root} if known else set(range(n))

    def swap(block, bit, senders):
        return lax.ppermute(block, axis, [(s, s ^ bit) for s in sorted(senders)])

    mine = pick(parts, side)
    if n > 1:
        got = swap(pick(parts, 1 - side), 1, holders)
        mine = jnp.where(root % 2 == side, mine, got)
        if known:
            holders = {root, root ^ 1}
    for bit in bits:
        got = swap(mine, bit, holders)
        mine = jnp.where((root & bit) == (me & bit), mine, got)
        if known:
            holders |= {h ^ bit for h in holders}
    if n == 1:
        return parts
    other = swap(mine, 1, holders)
    first = jnp.where(side == 0, mine, other)
    second = jnp.where(side == 0, other, mine)
    return jnp.stack([first, second])


def dot(a, b):
    return jnp.matmul(a, b, preferred_element_type=F32)


def make(rows_n, cols_n):
    def on_device(tile_u, tile_v, tile_ranks, inverses, panel_order):
        rows_here, cols_here = tile_u.shape[:2]
        rank = tile_u.shape[3]
        last_row = rows_n * rows_here - 1
        last_col = cols_n * cols_here - 1
        row_last_first = panel_order[0, 0] == last_row
        col_last_first = panel_order[0, 1] == last_col
        row_dyn = jnp.where(row_last_first, panel_order[1, 0], panel_order[0, 0])
        col_dyn = jnp.where(col_last_first, panel_order[1, 1], panel_order[0, 1])

        kept = jnp.arange(rank, dtype=jnp.int32)[None, None, :, None] < tile_ranks[:, :, None, None]
        right = jnp.where(kept, tile_v, jnp.zeros((), BF16))

        def by_row(tiles):
            fixed = spread(tiles[rows_here - 1], "row", rows_n, rows_n - 1)
            moving = spread(pick(tiles, row_dyn % rows_here), "row", rows_n, row_dyn // rows_here)
            return (jnp.where(row_last_first, fixed, moving), jnp.where(row_last_first, moving, fixed))

        def by_col(fixed, moving):
            fixed = spread(fixed, "col", cols_n, cols_n - 1)
            moving = spread(moving, "col", cols_n, col_dyn // cols_here)
            return (jnp.where(col_last_first, fixed, moving), jnp.where(col_last_first, moving, fixed))

        def panel(tiles):
            return by_col(tiles[:, cols_here - 1], pick(tiles, col_dyn % cols_here, 1))

        def halves(tile):
            return tile.reshape(2, tile.shape[0] // 2, tile.shape[1])

        def cross(one, two):
            for_last = jnp.where(col_last_first, two[cols_here - 1], one[cols_here - 1])
            local = col_dyn % cols_here
            for_dyn = jnp.where(col_last_first, pick(one, local), pick(two, local))
            a, b = by_col(halves(for_last), halves(for_dyn))
            return a.reshape(one.shape[1:]), b.reshape(one.shape[1:])

        up1, up2 = by_row(tile_u)
        vq1, vq2 = panel(right)
        u21, u12 = cross(up1, up2)
        vp1, vp2 = by_row(right)
        v21, v12 = cross(vp1, vp2)
        uq1, uq2 = panel(tile_u)

        wide = cols_here * rank
        s1 = dot(inverses[0], jnp.concatenate([up1[j] for j in range(cols_here)] + [u12], axis=1)).astype(BF16)
        s2 = dot(inverses[1], jnp.concatenate([up2[j] for j in range(cols_here)] + [u21], axis=1)).astype(BF16)
        tall = rows_here * rank
        c1 = dot(jnp.concatenate([vq1.reshape(tall, -1), v21]), s1).astype(BF16)
        c2 = dot(jnp.concatenate([vq2.reshape(tall, -1), v12]), s2).astype(BF16)

        row_global = lax.axis_index("row") * rows_here + jnp.arange(rows_here, dtype=jnp.int32)
        col_global = lax.axis_index("col") * cols_here + jnp.arange(cols_here, dtype=jnp.int32)
        p1, p2 = panel_order[0, 0], panel_order[1, 0]
        q1, q2 = panel_order[0, 1], panel_order[1, 1]
        open1 = (row_global != p1)[:, None] & (col_global != q1)[None, :]
        open2 = open1 & (row_global != p2)[:, None] & (col_global != q2)[None, :]
        m1 = open1.astype(F32)
        m2 = open2.astype(F32)

        def block(c, i, j):
            return c[i * rank:(i + 1) * rank, j * rank:(j + 1) * rank]

        outs = []
        for i in range(rows_here):
            line = []
            for j in range(cols_here):
                c1_p2j = block(c1, rows_here, j)
                c1_iq2 = block(c1, i, cols_here)
                below = jnp.concatenate([block(c2, rows_here, j), block(c2, rows_here, cols_here)], axis=1)
                low = -dot(c1_iq2, below)
                low_a, low_b = low[:, :rank], low[:, rank:].astype(BF16)
                high_a, high_b = block(c2, i, j), block(c2, i, cols_here)
                m_q1p1 = -m1[i, j] * block(c1, i, j).astype(F32) + m2[i, j] * dot(low_b, c1_p2j)
                m_q1p2 = -m2[i, j] * low_a
                m_q2p1 = m2[i, j] * dot(high_b, c1_p2j)
                m_q2p2 = -m2[i, j] * high_a.astype(F32)
                mix = jnp.concatenate([
                    jnp.concatenate([m_q1p1, m_q1p2], axis=1),
                    jnp.concatenate([m_q2p1, m_q2p2], axis=1)]).astype(BF16)
                change = dot(mix, jnp.concatenate([vp1[j], vp2[j]])).astype(BF16)
                line.append(jnp.concatenate([right[i, j], change]))
            outs.append(jnp.stack(line))
        right_all = jnp.stack(outs)
        left_all = jnp.concatenate([
            tile_u,
            jnp.broadcast_to(uq1[:, None], tile_u.shape),
            jnp.broadcast_to(uq2[:, None], tile_u.shape)], axis=3)
        return jnp.einsum("rcbk,rckd->rcbd", left_all, right_all, preferred_element_type=F32).astype(BF16)

    return on_device


def solution(mesh):
    placed = (P("row", "col", None, None), P("row", "col", None, None), P("row", "col"), P(), P())
    return jax.shard_map(
        make(mesh.shape["row"], mesh.shape["col"]),
        mesh=mesh,
        in_specs=placed,
        out_specs=P("row", "col", None, None),
        check_vma=False,
    )
```

time: 329 us -> 153 us (0.47)
  waiting for transfers between devices: 262 us -> 45.8 us
  starting transfers between devices: 0.13 us -> 50 us
  between operations: 22.7 us -> 9.69 us
  local copies, waits for them, and re-layouts: 6.75 us -> 11.1 us
    psum x4 -> x0, waiting for transfers between devices: 262 us -> none  [from_root(): return lax.psum(jnp.where(mine, value, jnp.zeros_like(value)), axis)]
    ppermute x0 -> x40, starting transfers between devices: none -> 50 us  [swap(): return lax.ppermute(block, axis, [(s, s ^ bit) for s in sorted(senders)])]
    ppermute x0 -> x40, waiting for transfers between devices: none -> 45.8 us  [swap(): return lax.ppermute(block, axis, [(s, s ^ bit) for s in sorted(senders)])]
    squeeze x0 -> x10, local copies, waits for them, and re-layouts: none -> 4.82 us  [the longest x9 3.76 us: pick(): return lax.dynamic_index_in_dim(array, index, axis, keepdims=False)]
    not x2 -> x0, other arithmetic: 3.52 us -> none  [advance(): jnp.logical_not(column_done)[None, :]]
    select_n x8 -> x34, other arithmetic: 8.24 us -> 9.04 us  [the longest x10 4.13 us: spread(): mine = jnp.where(root % 2 == side, mine, got)]
    dot_general x5 -> x19, matrix products: 23 us -> 22.2 us  [the longest x18 15.3 us: dot(): return jnp.matmul(a, b, preferred_element_type=F32)]
  transfers between devices with their start and end apart: 4 -> 40, of which waited for: 4 -> 13; matrix products, arithmetic and copies ran while one was open for 3% -> 12% of each run, Pallas kernels for 0% -> 0%
where the time goes in v1:
time: 153 us
  starting transfers between devices  50 us (33%)
  waiting for transfers between devices  45.8 us (30%)
  matrix products  22.2 us (15%)
  other arithmetic  13.7 us (9%)
  local copies, waits for them, and re-layouts  11.1 us (7%)
  between operations  9.69 us (6%)
    ppermute x40, starting transfers between devices, swap(): return lax.ppermute(block, axis, [(s, s ^ bit) for s in sorted(senders)])  50 us
    ppermute x40, waiting for transfers between devices, swap(): return lax.ppermute(block, axis, [(s, s ^ bit) for s in sorted(senders)])  45.8 us
    dot_general x18, matrix products, dot(): return jnp.matmul(a, b, preferred_element_type=F32)  15.3 us
    dot_general x1, matrix products, on_device(): jnp.einsum('rcbk,rckd->rcbd', left_all, right_all, preferred_element_type...  6.92 us
    select_n x10, other arithmetic, spread(): mine = jnp.where(root % 2 == side, mine, got)  4.13 us
    squeeze x9, local copies, waits for them, and re-layouts, pick(): return lax.dynamic_index_in_dim(array, index, axis, keepdims=False)  3.76 us
  transfers between devices with their start and end apart: 40, of which 13 were waited for; matrix products, arithmetic and copies ran while one was open for 12% of the time, Pallas kernels for 0%

profile of v1, /device:TPU:0, one launch (start us, length us, event | category | flops | bytes accessed | tf_op | source)
XLA Modules:
  0.0 152.5 jit_solution(150112694960844906)
XLA Ops:
  4.0 1.4 collective-permute-start
  10.7 2.9 %collective-permute-start.30 = (bf16[1024,128]{1,0:T(8,128)(2,1)}, bf16[1024,128]{1,0:T(8,128)(2,1)}, u32[]{:S(2)}, u32[]{:S(2)}) collective-permute-start(bf16[1024,128]{1,0:T(8,128)(2,1)} %get-tuple-element.19), channel_id=1, source_target_pairs={{0,4},{4,0},{8,12},{12,8},{16,20},{20,16},{24,28},{28,24},{1,5},{5... | collective-permute-start | bytes 786440 | tf_op jit(solution)/shard_map/ppermute | solution.py:24
  13.7 1.4 broadcast_select_fusion
  34.8 4.4 %collective-permute-done.12 = bf16[128,1024]{1,0:T(8,128)(2,1)S(1)} collective-permute-done((bf16[128,1024]{1,0:T(8,128)(2,1)}, bf16[128,1024]{1,0:T(8,128)(2,1)S(1)}, u32[]{:S(2)}, u32[]{:S(2)}) %collective-permute-start.12) | collective-permute-done | bytes 262176 | tf_op jit(solution)/shard_map/ppermute | solution.py:24
  40.5 1.6 %collective-permute-start.31 = (bf16[1024,128]{1,0:T(8,128)(2,1)S(1)}, bf16[1024,128]{1,0:T(8,128)(2,1)S(1)}, u32[]{:S(2)}, u32[]{:S(2)}) collective-permute-start(bf16[1024,128]{1,0:T(8,128)(2,1)S(1)} %get-tuple-element.17), channel_id=1, source_target_pairs={{0,8},{4,12},{8,0},{12,4},{16,24},{20,28},{24,16},{28,20},{1,9},{5... | collective-permute-start | bytes 786440 | tf_op jit(solution)/shard_map/ppermute | solution.py:24
  42.2 4.0 %collective-permute-start.4 = (bf16[1024,128]{1,0:T(8,128)(2,1)S(1)}, bf16[1024,128]{1,0:T(8,128)(2,1)S(1)}, u32[]{:S(2)}, u32[]{:S(2)}) collective-permute-start(bf16[1024,128]{1,0:T(8,128)(2,1)S(1)} %get-tuple-element.18), channel_id=1, source_target_pairs={{0,2},{1,3},{2,0},{3,1},{4,6},{5,7},{6,4},{7,5},{8,10},{9,11},{10,... | collective-permute-start | bytes 786440 | tf_op jit(solution)/shard_map/ppermute | solution.py:24
  49.3 2.7 %collective-permute-start.10 = (bf16[128,1024]{1,0:T(8,128)(2,1)S(1)}, bf16[128,1024]{1,0:T(8,128)(2,1)S(1)}, u32[]{:S(2)}, u32[]{:S(2)}) collective-permute-start(bf16[128,1024]{1,0:T(8,128)(2,1)S(1)} %get-tuple-element.21), channel_id=1, source_target_pairs={{0,2},{1,3},{2,0},{3,1},{4,6},{5,7},{6,4},{7,5},{8,10},{9,11},{10,... | collective-permute-start | bytes 786440 | tf_op jit(solution)/shard_map/ppermute | solution.py:24
  52.1 13.4 %collective-permute-start.13 = (bf16[128,1024]{1,0:T(8,128)(2,1)S(1)}, bf16[128,1024]{1,0:T(8,128)(2,1)S(1)}, u32[]{:S(2)}, u32[]{:S(2)}) collective-permute-start(bf16[128,1024]{1,0:T(8,128)(2,1)S(1)} %get-tuple-element.22), channel_id=1, source_target_pairs={{0,8},{4,12},{8,0},{12,4},{16,24},{20,28},{24,16},{28,20},{1,9},{5... | collective-permute-start | bytes 786440 | tf_op jit(solution)/shard_map/ppermute | solution.py:24
  67.9 10.0 %collective-permute-done.13 = bf16[128,1024]{1,0:T(8,128)(2,1)S(1)} collective-permute-done((bf16[128,1024]{1,0:T(8,128)(2,1)S(1)}, bf16[128,1024]{1,0:T(8,128)(2,1)S(1)}, u32[]{:S(2)}, u32[]{:S(2)}) %collective-permute-start.13) | collective-permute-done | bytes 262176 | tf_op jit(solution)/shard_map/ppermute | solution.py:24
  79.9 4.0 %collective-permute-done.28 = bf16[1024,128]{1,0:T(8,128)(2,1)S(1)} collective-permute-done((bf16[1024,128]{1,0:T(8,128)(2,1)S(1)}, bf16[1024,128]{1,0:T(8,128)(2,1)S(1)}, u32[]{:S(2)}, u32[]{:S(2)}) %collective-permute-start.28) | collective-permute-done | bytes 262176 | tf_op jit(solution)/shard_map/ppermute | solution.py:24
  84.6 6.6 %collective-permute-done.18 = bf16[128,1024]{1,0:T(8,128)(2,1)S(1)} collective-permute-done((bf16[128,1024]{1,0:T(8,128)(2,1)S(1)}, bf16[128,1024]{1,0:T(8,128)(2,1)S(1)}, u32[]{:S(2)}, u32[]{:S(2)}) %collective-permute-start.18) | collective-permute-done | bytes 262176 | tf_op jit(solution)/shard_map/ppermute | solution.py:24
  91.2 1.4 collective-permute-start.33
  92.7 2.9 %collective-permute-done.14 = bf16[128,1024]{1,0:T(8,128)(2,1)S(1)} collective-permute-done((bf16[128,1024]{1,0:T(8,128)(2,1)S(1)}, bf16[128,1024]{1,0:T(8,128)(2,1)S(1)}, u32[]{:S(2)}, u32[]{:S(2)}) %collective-permute-start.14) | collective-permute-done | bytes 262176 | tf_op jit(solution)/shard_map/ppermute | solution.py:24
  98.1 2.4 %collective-permute-done.33 = bf16[1024,128]{1,0:T(8,128)(2,1)S(1)} collective-permute-done((bf16[1024,128]{1,0:T(8,128)(2,1)S(1)}, bf16[1024,128]{1,0:T(8,128)(2,1)S(1)}, u32[]{:S(2)}, u32[]{:S(2)}) %collective-permute-start.33) | collective-permute-done | bytes 262176 | tf_op jit(solution)/shard_map/ppermute | solution.py:24
  102.4 3.7 %collective-permute-done.19 = bf16[128,1024]{1,0:T(8,128)(2,1)S(1)} collective-permute-done((bf16[128,1024]{1,0:T(8,128)(2,1)S(1)}, bf16[128,1024]{1,0:T(8,128)(2,1)S(1)}, u32[]{:S(2)}, u32[]{:S(2)}) %collective-permute-start.19) | collective-permute-done | bytes 262176 | tf_op jit(solution)/shard_map/ppermute | solution.py:24
  106.1 3.2 %collective-permute-done.15 = bf16[128,1024]{1,0:T(8,128)(2,1)S(1)} collective-permute-done((bf16[128,1024]{1,0:T(8,128)(2,1)S(1)}, bf16[128,1024]{1,0:T(8,128)(2,1)S(1)}, u32[]{:S(2)}, u32[]{:S(2)}) %collective-permute-start.15) | collective-permute-done | bytes 262176 | tf_op jit(solution)/shard_map/ppermute | solution.py:24
  113.3 2.7 %collective-permute-start.24 = (bf16[64,1024]{1,0:T(8,128)(2,1)S(1)}, bf16[64,1024]{1,0:T(8,128)(2,1)S(1)}, u32[]{:S(2)}, u32[]{:S(2)}) collective-permute-start(bf16[64,1024]{1,0:T(8,128)(2,1)S(1)} %bitcast_select_fusion.10), channel_id=1, source_target_pairs={{0,2},{1,3},{2,0},{3,1},{4,6},{5,7},{6,4},{7,5},{8,10},{9,11},{10,... | collective-permute-start | bytes 393224 | tf_op jit(solution)/shard_map/ppermute | solution.py:24
  116.0 1.5 collective-permute-start.21
  117.9 2.3 %collective-permute-done.38 = bf16[512,128]{1,0:T(8,128)(2,1)S(1)} collective-permute-done((bf16[512,128]{1,0:T(8,128)(2,1)S(1)}, bf16[512,128]{1,0:T(8,128)(2,1)S(1)}, u32[]{:S(2)}, u32[]{:S(2)}) %collective-permute-start.38) | collective-permute-done | bytes 131104 | tf_op jit(solution)/shard_map/ppermute | solution.py:24
  120.3 2.7 %collective-permute-done.24 = bf16[64,1024]{1,0:T(8,128)(2,1)S(1)} collective-permute-done((bf16[64,1024]{1,0:T(8,128)(2,1)S(1)}, bf16[64,1024]{1,0:T(8,128)(2,1)S(1)}, u32[]{:S(2)}, u32[]{:S(2)}) %collective-permute-start.24) | collective-permute-done | bytes 131104 | tf_op jit(solution)/shard_map/ppermute | solution.py:24
  123.1 2.6 %collective-permute-done.21 = bf16[64,1024]{1,0:T(8,128)(2,1)S(1)} collective-permute-done((bf16[64,1024]{1,0:T(8,128)(2,1)S(1)}, bf16[64,1024]{1,0:T(8,128)(2,1)S(1)}, u32[]{:S(2)}, u32[]{:S(2)}) %collective-permute-start.21) | collective-permute-done | bytes 131104 | tf_op jit(solution)/shard_map/ppermute | solution.py:24
  128.0 4.1 %convolution_convert_fusion.6 = bf16[384,384]{0,1:T(8,128)(2,1)} fusion(bf16[2,1024,1024]{2,1,0:T(8,128)(2,1)} %param.8, bf16[128,1024]{1,0:T(8,128)(2,1)} %bitcast.181, bf16[256,1024]{1,0:T(8,128)(2,1)S(1)} %bitcast.177, bf16[1024,128]{1,0:T(8,128)(2,1)} %bitcast.179, bf16[1024,128]{1,0:T(8,128)(2,1)} %get-tuple-element.38, ...), kind=kOutput, calls=%fused_computation.24 | convolution fusion | flops 1111769088 | bytes 3964928 | tf_op jit(solution)/shard_map/dot_general | solution.py:46
  132.1 3.4 %convolution_convert_fusion.5 = bf16[384,384]{0,1:T(8,128)(2,1)S(1)} fusion(bf16[2,1024,1024]{2,1,0:T(8,128)(2,1)} %param.8, bf16[128,1024]{1,0:T(8,128)(2,1)} %bitcast.180, bf16[256,1024]{1,0:T(8,128)(2,1)S(1)} %bitcast.176, bf16[1024,128]{1,0:T(8,128)(2,1)} %bitcast.178, bf16[1024,128]{1,0:T(8,128)(2,1)} %get-tuple-element.37, ...), kind=kOutput, calls=%fused_computation.23 | convolution fusion | flops 1111769088 | bytes 3964928 | tf_op jit(solution)/shard_map/dot_general | solution.py:46
  145.6 6.9 %convolution_convert_fusion = bf16[2,2,1024,1024]{3,2,1,0:T(8,128)(2,1)} fusion(bf16[2,2,1024,128]{3,2,1,0:T(8,128)(2,1)S(1)} %broadcast_in_dim.17, bf16[2,2,1024,128]{3,2,1,0:T(8,128)(2,1)S(1)} %broadcast_in_dim.16, bf16[2,2,1024,128]{3,2,1,0:T(8,128)(2,1)S(1)} %copy-done, bf16[1,2,384,1024]{3,2,1,0:T(8,128)(2,1)S(1)} %maximum_bitcast_fusion.1, ...), kind=kOutput, calls=%fused_computation | convolution fusion | flops 3236429824 | bytes 14680064 | tf_op jit(solution)/shard_map/rcbk,rckd->rcbd/dot_general | solution.py:137
  (189 shorter events, 50.7 us)
Async XLA Ops:
  1.9 29.4 %collective-permute-start.26 = (bf16[1024,128]{1,0:T(8,128)(2,1)}, bf16[1024,128]{1,0:T(8,128)(2,1)}, u32[]{:S(2)}, u32[]{:S(2)}) collective-permute-start(bf16[1024,128]{1,0:T(8,128)(2,1)} %dynamic-slice_bitcast_fusion.1), channel_id=1, source_target_pairs={{28,24},{29,25},{30,26},{31,27}} | collective-permute-start | bytes 786440 | tf_op jit(solution)/shard_map/ppermute | solution.py:24
  4.0 29.0 %collective-permute-start = (bf16[1024,128]{1,0:T(8,128)(2,1)}, bf16[1024,128]{1,0:T(8,128)(2,1)}, u32[]{:S(2)}, u32[]{:S(2)}) collective-permute-start(bf16[1024,128]{1,0:T(8,128)(2,1)} %dynamic-slice_bitcast_fusion.7), channel_id=1, source_target_pairs={{3,2},{7,6},{11,10},{15,14},{19,18},{23,22},{27,26},{31,30}} | collective-permute-start | bytes 786440 | tf_op jit(solution)/shard_map/ppermute | solution.py:24
  10.7 18.7 %collective-permute-start.30 = (bf16[1024,128]{1,0:T(8,128)(2,1)}, bf16[1024,128]{1,0:T(8,128)(2,1)}, u32[]{:S(2)}, u32[]{:S(2)}) collective-permute-start(bf16[1024,128]{1,0:T(8,128)(2,1)} %get-tuple-element.19), channel_id=1, source_target_pairs={{0,4},{4,0},{8,12},{12,8},{16,20},{20,16},{24,28},{28,24},{1,5},{5... | collective-permute-start | bytes 786440 | tf_op jit(solution)/shard_map/ppermute | solution.py:24
  13.7 16.6 %collective-permute-start.3 = (bf16[1024,128]{1,0:T(8,128)(2,1)}, bf16[1024,128]{1,0:T(8,128)(2,1)}, u32[]{:S(2)}, u32[]{:S(2)}) collective-permute-start(bf16[1024,128]{1,0:T(8,128)(2,1)} %get-tuple-element.20), channel_id=1, source_target_pairs={{0,1},{1,0},{2,3},{3,2},{4,5},{5,4},{6,7},{7,6},{8,9},{9,8},{10,11... | collective-permute-start | bytes 786440 | tf_op jit(solution)/shard_map/ppermute | solution.py:24
  16.7 25.6 %collective-permute-start.16 = (bf16[128,1024]{1,0:T(8,128)(2,1)}, bf16[128,1024]{1,0:T(8,128)(2,1)}, u32[]{:S(2)}, u32[]{:S(2)}) collective-permute-start(bf16[128,1024]{1,0:T(8,128)(2,1)} %dynamic-slice_bitcast_fusion.2), channel_id=1, source_target_pairs={{28,24},{29,25},{30,26},{31,27}} | collective-permute-start | bytes 786440 | tf_op jit(solution)/shard_map/ppermute | solution.py:24
  29.4 17.8 %collective-permute-start.6 = (bf16[128,1024]{1,0:T(8,128)(2,1)}, bf16[128,1024]{1,0:T(8,128)(2,1)S(1)}, u32[]{:S(2)}, u32[]{:S(2)}) collective-permute-start(bf16[128,1024]{1,0:T(8,128)(2,1)} %dynamic-slice_bitcast_fusion.5), channel_id=1, source_target_pairs={{3,2},{7,6},{11,10},{15,14},{19,18},{23,22},{27,26},{31,30}} | collective-permute-start | bytes 786440 | tf_op jit(solution)/shard_map/ppermute | solution.py:24
  33.0 14.9 %collective-permute-start.27 = (bf16[1024,128]{1,0:T(8,128)(2,1)S(1)}, bf16[1024,128]{1,0:T(8,128)(2,1)S(1)}, u32[]{:S(2)}, u32[]{:S(2)}) collective-permute-start(bf16[1024,128]{1,0:T(8,128)(2,1)S(1)} %bitcast_select_fusion.1), channel_id=1, source_target_pairs={{24,8},{28,12},{25,9},{29,13},{26,10},{30,14},{27,11},{31,15}} | collective-permute-start | bytes 786440 | tf_op jit(solution)/shard_map/ppermute | solution.py:24
  39.2 12.8 %collective-permute-start.1 = (bf16[1024,128]{1,0:T(8,128)(2,1)S(1)}, bf16[1024,128]{1,0:T(8,128)(2,1)S(1)}, u32[]{:S(2)}, u32[]{:S(2)}) collective-permute-start(bf16[1024,128]{1,0:T(8,128)(2,1)S(1)} %bitcast_select_fusion.7), channel_id=1, source_target_pairs={{2,0},{3,1},{6,4},{7,5},{10,8},{11,9},{14,12},{15,13},{18,16},{19,... | collective-permute-start | bytes 786440 | tf_op jit(solution)/shard_map/ppermute | solution.py:24
  40.5 26.3 %collective-permute-start.31 = (bf16[1024,128]{1,0:T(8,128)(2,1)S(1)}, bf16[1024,128]{1,0:T(8,128)(2,1)S(1)}, u32[]{:S(2)}, u32[]{:S(2)}) collective-permute-start(bf16[1024,128]{1,0:T(8,128)(2,1)S(1)} %get-tuple-element.17), channel_id=1, source_target_pairs={{0,8},{4,12},{8,0},{12,4},{16,24},{20,28},{24,16},{28,20},{1,9},{5... | collective-permute-start | bytes 786440 | tf_op jit(solution)/shard_map/ppermute | solution.py:24
  42.2 24.7 %collective-permute-start.4 = (bf16[1024,128]{1,0:T(8,128)(2,1)S(1)}, bf16[1024,128]{1,0:T(8,128)(2,1)S(1)}, u32[]{:S(2)}, u32[]{:S(2)}) collective-permute-start(bf16[1024,128]{1,0:T(8,128)(2,1)S(1)} %get-tuple-element.18), channel_id=1, source_target_pairs={{0,2},{1,3},{2,0},{3,1},{4,6},{5,7},{6,4},{7,5},{8,10},{9,11},{10,... | collective-permute-start | bytes 786440 | tf_op jit(solution)/shard_map/ppermute | solution.py:24
  48.0 17.5 %collective-permute-start.7 = (bf16[128,1024]{1,0:T(8,128)(2,1)S(1)}, bf16[128,1024]{1,0:T(8,128)(2,1)S(1)}, u32[]{:S(2)}, u32[]{:S(2)}) collective-permute-start(bf16[128,1024]{1,0:T(8,128)(2,1)S(1)} %bitcast_select_fusion.5), channel_id=1, source_target_pairs={{2,0},{3,1},{6,4},{7,5},{10,8},{11,9},{14,12},{15,13},{18,16},{19,... | collective-permute-start | bytes 786440 | tf_op jit(solution)/shard_map/ppermute | solution.py:24
  49.3 18.5 %collective-permute-start.10 = (bf16[128,1024]{1,0:T(8,128)(2,1)S(1)}, bf16[128,1024]{1,0:T(8,128)(2,1)S(1)}, u32[]{:S(2)}, u32[]{:S(2)}) collective-permute-start(bf16[128,1024]{1,0:T(8,128)(2,1)S(1)} %get-tuple-element.21), channel_id=1, source_target_pairs={{0,2},{1,3},{2,0},{3,1},{4,6},{5,7},{6,4},{7,5},{8,10},{9,11},{10,... | collective-permute-start | bytes 786440 | tf_op jit(solution)/shard_map/ppermute | solution.py:24
  52.1 25.8 %collective-permute-start.13 = (bf16[128,1024]{1,0:T(8,128)(2,1)S(1)}, bf16[128,1024]{1,0:T(8,128)(2,1)S(1)}, u32[]{:S(2)}, u32[]{:S(2)}) collective-permute-start(bf16[128,1024]{1,0:T(8,128)(2,1)S(1)} %get-tuple-element.22), channel_id=1, source_target_pairs={{0,8},{4,12},{8,0},{12,4},{16,24},{20,28},{24,16},{28,20},{1,9},{5... | collective-permute-start | bytes 786440 | tf_op jit(solution)/shard_map/ppermute | solution.py:24
  65.5 18.4 %collective-permute-start.28 = (bf16[1024,128]{1,0:T(8,128)(2,1)S(1)}, bf16[1024,128]{1,0:T(8,128)(2,1)S(1)}, u32[]{:S(2)}, u32[]{:S(2)}) collective-permute-start(bf16[1024,128]{1,0:T(8,128)(2,1)S(1)} %broadcast_select_fusion.14), channel_id=1, source_target_pairs={{8,0},{12,4},{24,16},{28,20},{9,1},{13,5},{25,17},{29,21},{10,2},{... | collective-permute-start | bytes 786440 | tf_op jit(solution)/shard_map/ppermute | solution.py:24
  66.9 12.3 %collective-permute-start.2 = (bf16[1024,128]{1,0:T(8,128)(2,1)S(1)}, bf16[1024,128]{1,0:T(8,128)(2,1)S(1)}, u32[]{:S(2)}, u32[]{:S(2)}) collective-permute-start(bf16[1024,128]{1,0:T(8,128)(2,1)S(1)} %broadcast_select_fusion.26), channel_id=1, source_target_pairs={{0,1},{1,0},{2,3},{3,2},{4,5},{5,4},{6,7},{7,6},{8,9},{9,8},{10,11... | collective-permute-start | bytes 786440 | tf_op jit(solution)/shard_map/ppermute | solution.py:24
  67.0 17.0 %collective-permute-start.32 = (bf16[1024,128]{1,0:T(8,128)(2,1)S(1)}, bf16[1024,128]{1,0:T(8,128)(2,1)S(1)}, u32[]{:S(2)}, u32[]{:S(2)}) collective-permute-start(bf16[1024,128]{1,0:T(8,128)(2,1)S(1)} %broadcast_select_fusion.12), channel_id=1, source_target_pairs={{0,16},{4,20},{8,24},{12,28},{16,0},{20,4},{24,8},{28,12},{1,17},{... | collective-permute-start | bytes 786440 | tf_op jit(solution)/shard_map/ppermute | solution.py:24
  67.8 11.5 %collective-permute-start.5 = (bf16[1024,128]{1,0:T(8,128)(2,1)S(1)}, bf16[1024,128]{1,0:T(8,128)(2,1)S(1)}, u32[]{:S(2)}, u32[]{:S(2)}) collective-permute-start(bf16[1024,128]{1,0:T(8,128)(2,1)S(1)} %broadcast_select_fusion.25), channel_id=1, source_target_pairs={{0,1},{1,0},{2,3},{3,2},{4,5},{5,4},{6,7},{7,6},{8,9},{9,8},{10,11... | collective-permute-start | bytes 786440 | tf_op jit(solution)/shard_map/ppermute | solution.py:24
  77.8 13.4 %collective-permute-start.18 = (bf16[128,1024]{1,0:T(8,128)(2,1)S(1)}, bf16[128,1024]{1,0:T(8,128)(2,1)S(1)}, u32[]{:S(2)}, u32[]{:S(2)}) collective-permute-start(bf16[128,1024]{1,0:T(8,128)(2,1)S(1)} %broadcast_select_fusion.16), channel_id=1, source_target_pairs={{8,0},{12,4},{24,16},{28,20},{9,1},{13,5},{25,17},{29,21},{10,2},{... | collective-permute-start | bytes 786440 | tf_op jit(solution)/shard_map/ppermute | solution.py:24
  79.2 17.6 %collective-permute-start.8 = (bf16[128,1024]{1,0:T(8,128)(2,1)S(1)}, bf16[128,1024]{1,0:T(8,128)(2,1)S(1)}, u32[]{:S(2)}, u32[]{:S(2)}) collective-permute-start(bf16[128,1024]{1,0:T(8,128)(2,1)S(1)} %broadcast_select_fusion.24), channel_id=1, source_target_pairs={{0,1},{1,0},{2,3},{3,2},{4,5},{5,4},{6,7},{7,6},{8,9},{9,8},{10,11... | collective-permute-start | bytes 786440 | tf_op jit(solution)/shard_map/ppermute | solution.py:24
  79.3 18.4 %collective-permute-start.11 = (bf16[128,1024]{1,0:T(8,128)(2,1)S(1)}, bf16[128,1024]{1,0:T(8,128)(2,1)S(1)}, u32[]{:S(2)}, u32[]{:S(2)}) collective-permute-start(bf16[128,1024]{1,0:T(8,128)(2,1)S(1)} %broadcast_select_fusion.23), channel_id=1, source_target_pairs={{0,1},{1,0},{2,3},{3,2},{4,5},{5,4},{6,7},{7,6},{8,9},{9,8},{10,11... | collective-permute-start | bytes 786440 | tf_op jit(solution)/shard_map/ppermute | solution.py:24
  83.9 11.7 %collective-permute-start.14 = (bf16[128,1024]{1,0:T(8,128)(2,1)S(1)}, bf16[128,1024]{1,0:T(8,128)(2,1)S(1)}, u32[]{:S(2)}, u32[]{:S(2)}) collective-permute-start(bf16[128,1024]{1,0:T(8,128)(2,1)S(1)} %broadcast_select_fusion.18), channel_id=1, source_target_pairs={{0,16},{4,20},{8,24},{12,28},{16,0},{20,4},{24,8},{28,12},{1,17},{... | collective-permute-start | bytes 786440 | tf_op jit(solution)/shard_map/ppermute | solution.py:24
  84.0 14.1 %collective-permute-start.29 = (bf16[1024,128]{1,0:T(8,128)(2,1)S(1)}, bf16[1024,128]{1,0:T(8,128)(2,1)S(1)}, u32[]{:S(2)}, u32[]{:S(2)}) collective-permute-start(bf16[1024,128]{1,0:T(8,128)(2,1)S(1)} %broadcast_select_fusion.15), channel_id=1, source_target_pairs={{0,4},{4,0},{8,12},{12,8},{16,20},{20,16},{24,28},{28,24},{1,5},{5... | collective-permute-start | bytes 786440 | tf_op jit(solution)/shard_map/ppermute | solution.py:24
  95.6 10.5 %collective-permute-start.19 = (bf16[128,1024]{1,0:T(8,128)(2,1)S(1)}, bf16[128,1024]{1,0:T(8,128)(2,1)S(1)}, u32[]{:S(2)}, u32[]{:S(2)}) collective-permute-start(bf16[128,1024]{1,0:T(8,128)(2,1)S(1)} %broadcast_select_fusion.17), channel_id=1, source_target_pairs={{0,4},{4,0},{8,12},{12,8},{16,20},{20,16},{24,28},{28,24},{1,5},{5... | collective-permute-start | bytes 786440 | tf_op jit(solution)/shard_map/ppermute | solution.py:24
  96.8 12.5 %collective-permute-start.15 = (bf16[128,1024]{1,0:T(8,128)(2,1)S(1)}, bf16[128,1024]{1,0:T(8,128)(2,1)S(1)}, u32[]{:S(2)}, u32[]{:S(2)}) collective-permute-start(bf16[128,1024]{1,0:T(8,128)(2,1)S(1)} %broadcast_select_fusion.19), channel_id=1, source_target_pairs={{0,4},{4,0},{8,12},{12,8},{16,20},{20,16},{24,28},{28,24},{1,5},{5... | collective-permute-start | bytes 786440 | tf_op jit(solution)/shard_map/ppermute | solution.py:24
  (32 other events, 188.4 us)

commit v2 on v0

v2 whole, which is shorter than its diff:
```python
import jax
import jax.numpy as jnp
from jax import lax
from jax.experimental import pallas as pl
from jax.experimental.pallas import tpu as pltpu
from jax.sharding import PartitionSpec as P

F32 = jnp.float32
BF16 = jnp.bfloat16
VMEM_BYTES = 48 * 1024 * 1024
WHOLE = pl.BlockSpec(memory_space=pltpu.VMEM)
SCALARS = pl.BlockSpec(memory_space=pltpu.SMEM)


def params():
    return pltpu.CompilerParams(vmem_limit_bytes=VMEM_BYTES)


def dot(a, b):
    return jnp.dot(a, b, preferred_element_type=F32)


def swap(block, axis, n, bit, senders=None):
    if senders is None:
        pairs = [(s, s ^ bit) for s in range(n)]
    else:
        used = set(senders) | {s ^ bit for s in senders}
        pairs = [(s, s ^ bit) for s in sorted(senders)]
        pairs += [(d, d) for d in range(n) if d not in used]
    return lax.ppermute(block, axis, pairs)


def upper_bits(n):
    return [1 << b for b in range(1, n.bit_length() - 1)]


def lanes_moving(keep, give, axis, n, root):
    me = lax.axis_index(axis)
    got = swap(give, axis, n, 1)
    mine = jnp.where(((root ^ me) & 1) == 0, keep, got)
    for bit in upper_bits(n):
        got = swap(mine, axis, n, bit)
        mine = jnp.where(((root ^ me) & bit) == 0, mine, got)
    return mine


def lanes_fixed(keep, give, axis, n):
    me = lax.axis_index(axis)
    root = n - 1
    got = swap(give, axis, n, 1, {root})
    mine = jnp.where(me == (root ^ 1), got, keep)
    holders = {root, root ^ 1}
    for bit in upper_bits(n)[::-1]:
        got = swap(mine, axis, n, bit, holders)
        mine = jnp.where(((root ^ me) & bit) == 0, mine, got)
        holders |= {h ^ bit for h in holders}
    return mine


def prep_kernel(info, ranks, u, v, *outs):
    (rs_uk, rs_ug, rd_uk, rd_ug, rs_vk, rs_vg, rd_vk, rd_vg, cs_k, cs_g, cd_k, cd_g) = outs
    rows, cols = u.shape[:2]
    rank, width = v.shape[2:]
    row_dyn, col_dyn, row_side, col_side = info[0], info[1], info[2], info[3]

    def kept(i, j):
        row = lax.broadcasted_iota(jnp.int32, (rank, width), 0)
        return jnp.where(row < ranks[i, j], v[i, j], jnp.zeros((), v.dtype))

    for i, (u_outs, v_outs) in ((rows - 1, ((rs_uk, rs_ug), (rs_vk, rs_vg))), (row_dyn, ((rd_uk, rd_ug), (rd_vk, rd_vg)))):
        for slot, j in enumerate((row_side, 1 - row_side)):
            u_outs[slot][...] = u[i, j]
            v_outs[slot][...] = kept(i, j)
    for j, outs_here in ((cols - 1, (cs_k, cs_g)), (col_dyn, (cd_k, cd_g))):
        for slot, i in enumerate((col_side, 1 - col_side)):
            outs_here[slot][0] = u[i, j]
            value = kept(i, j)
            for k in range(width // rank):
                outs_here[slot][1, k * rank:(k + 1) * rank, :] = value[:, k * rank:(k + 1) * rank]


def solve_kernel(inverses, *refs):
    tiles, out = refs[:-1], refs[-1]
    per = len(tiles) // 2
    rank = tiles[0].shape[1]
    for s in range(2):
        joined = jnp.concatenate([t[...] for t in tiles[s * per:(s + 1) * per]], axis=1)
        out[s] = dot(inverses[s], joined).astype(BF16)


def core_kernel(solved, q1, q2, v21, v12, out):
    rank = v21.shape[0]
    count = v21.shape[1] // rank
    for s, (panel, more) in enumerate(((q1, v21), (q2, v12))):
        rows = panel.shape[0]
        lines = [jnp.concatenate([panel[i, k * rank:(k + 1) * rank, :] for k in range(count)], axis=1) for i in range(rows)]
        tall = jnp.concatenate(lines + [more[...]], axis=0)
        out[s] = dot(tall, solved[s]).astype(BF16)


def final_kernel(info, ranks, u, v, uq1, uq2, vp1, vp2, cores, out):
    i, j = pl.program_id(0), pl.program_id(1)
    rank, width = v.shape[2:]
    rows_here, cols_here = pl.num_programs(0), pl.num_programs(1)
    row, col = info[0] + i, info[1] + j
    open1 = jnp.logical_and(row != info[2], col != info[4])
    open2 = jnp.logical_and(open1, jnp.logical_and(row != info[3], col != info[5]))
    m1 = jnp.where(open1, F32(1), F32(0))
    m2 = jnp.where(open2, F32(1), F32(0))
    edge_r, edge_c = cores.shape[1] - rank, cores.shape[2] - rank
    top, left = pl.ds(pl.multiple_of(i * rank, rank), rank), pl.ds(pl.multiple_of(j * rank, rank), rank)
    foot, side = pl.ds(edge_r, rank), pl.ds(edge_c, rank)
    c1_ij, c1_iq2, c1_p2j = cores[0, top, left], cores[0, top, side], cores[0, foot, left]
    high_a, high_b = cores[1, top, left], cores[1, top, side]
    low_a = -dot(c1_iq2, cores[1, foot, left])
    low_b = -dot(c1_iq2, cores[1, foot, side])
    q1p1 = m2 * dot(low_b.astype(BF16), c1_p2j) - m1 * c1_ij.astype(F32)
    q2p1 = m2 * dot(high_b, c1_p2j)
    mix = jnp.concatenate([
        jnp.concatenate([q1p1, -m2 * low_a], axis=1),
        jnp.concatenate([q2p1, -m2 * high_a.astype(F32)], axis=1)], axis=0).astype(BF16)
    change = dot(mix, jnp.concatenate([vp1[0], vp2[0]], axis=0)).astype(BF16)
    line = lax.broadcasted_iota(jnp.int32, (rank, width), 0)
    own = jnp.where(line < ranks[i, j], v[0, 0], jnp.zeros((), BF16))
    right = jnp.concatenate([own, change], axis=0)
    out[0, 0] = dot(jnp.concatenate([u[0, 0], uq1[0], uq2[0]], axis=1), right).astype(BF16)


def make(rows_n, cols_n):
    def on_device(tile_u, tile_v, tile_ranks, inverses, panel_order):
        rows, cols, width, rank = tile_u.shape
        me_row, me_col = lax.axis_index("row"), lax.axis_index("col")
        p1, p2 = panel_order[0, 0], panel_order[1, 0]
        q1, q2 = panel_order[0, 1], panel_order[1, 1]
        row_first = p1 == rows_n * rows - 1
        col_first = q1 == cols_n * cols - 1
        row_dyn = jnp.where(row_first, p2, p1)
        col_dyn = jnp.where(col_first, q2, q1)
        side_r, side_c = me_row % 2, me_col % 2

        tall = jax.ShapeDtypeStruct((width, rank), BF16)
        flat = jax.ShapeDtypeStruct((rank, width), BF16)
        pair = jax.ShapeDtypeStruct((2, width, rank), BF16)
        cut = pl.pallas_call(
            prep_kernel,
            out_shape=[tall] * 4 + [flat] * 4 + [pair] * 4,
            in_specs=[SCALARS, SCALARS, WHOLE, WHOLE],
            out_specs=[WHOLE] * 12,
            compiler_params=params(),
        )(jnp.stack([row_dyn % rows, col_dyn % cols, side_r, side_c]).astype(jnp.int32), tile_ranks, tile_u, tile_v)
        rs_uk, rs_ug, rd_uk, rd_ug, rs_vk, rs_vg, rd_vk, rd_vg, cs_k, cs_g, cd_k, cd_g = cut

        def by_row(fixed_keep, fixed_give, moving_keep, moving_give):
            fixed = lanes_fixed(fixed_keep, fixed_give, "row", rows_n)
            moving = lanes_moving(moving_keep, moving_give, "row", rows_n, row_dyn // rows)
            mine = jnp.stack([jnp.where(row_first, fixed, moving), jnp.where(row_first, moving, fixed)])
            other = swap(mine, "row", rows_n, 1)
            return [jnp.stack([jnp.where(side_r == 0, mine[s], other[s]), jnp.where(side_r == 0, other[s], mine[s])]) for s in range(2)]

        def cross(one, two):
            shape = one.shape[1:]
            cand = jnp.stack([jnp.where(q1 % cols == 0, two[0], two[1]), jnp.where(q2 % cols == 0, one[0], one[1])])
            cand = cand.reshape(2, 2, shape[0] // 2, shape[1])
            keep = jnp.where(side_c == 0, cand[:, 0], cand[:, 1])
            give = jnp.where(side_c == 0, cand[:, 1], cand[:, 0])
            root = jnp.stack([q1 // cols, q2 // cols])[:, None, None]
            mine = lanes_moving(keep, give, "col", cols_n, root)
            other = swap(mine, "col", cols_n, 1)
            first, second = jnp.where(side_c == 0, mine, other), jnp.where(side_c == 0, other, mine)
            both = jnp.concatenate([first, second], axis=1)
            return both[0], both[1]

        up1, up2 = by_row(rs_uk, rs_ug, rd_uk, rd_ug)
        fixed = lanes_fixed(cs_k, cs_g, "col", cols_n)
        moving = lanes_moving(cd_k, cd_g, "col", cols_n, col_dyn // cols)
        mine = jnp.stack([jnp.where(col_first, fixed, moving), jnp.where(col_first, moving, fixed)])
        other = swap(mine, "col", cols_n, 1)
        first, second = jnp.where(side_c == 0, mine, other), jnp.where(side_c == 0, other, mine)
        uq1, uq2 = (jnp.stack([first[s, 0], second[s, 0]]) for s in range(2))
        vq1, vq2 = (jnp.stack([first[s, 1], second[s, 1]]) for s in range(2))
        u21, u12 = cross(up1, up2)
        vp1, vp2 = by_row(rs_vk, rs_vg, rd_vk, rd_vg)
        v21, v12 = cross(vp1, vp2)

        solved = pl.pallas_call(
            solve_kernel,
            out_shape=jax.ShapeDtypeStruct((2, width, 3 * rank), BF16),
            in_specs=[WHOLE] * 7,
            out_specs=WHOLE,
            compiler_params=params(),
            cost_estimate=pl.CostEstimate(flops=12 * width * width * rank, bytes_accessed=16 * width * rank + 4 * width * width, transcendentals=0),
        )(inverses, up1[0], up1[1], u12, up2[0], up2[1], u21)
        cores = pl.pallas_call(
            core_kernel,
            out_shape=jax.ShapeDtypeStruct((2, 3 * rank, 3 * rank), BF16),
            in_specs=[WHOLE] * 5,
            out_specs=WHOLE,
            compiler_params=params(),
        )(solved, vq1, vq2, v21, v12)

        info = jnp.stack([me_row * rows, me_col * cols, p1, p2, q1, q2]).astype(jnp.int32)
        return pl.pallas_call(
            final_kernel,
            out_shape=jax.ShapeDtypeStruct((rows, cols, width, width), BF16),
            grid=(rows, cols),
            in_specs=[
                SCALARS, SCALARS,
                pl.BlockSpec((1, 1, width, rank), lambda i, j: (i, j, 0, 0)),
                pl.BlockSpec((1, 1, rank, width), lambda i, j: (i, j, 0, 0)),
                pl.BlockSpec((1, width, rank), lambda i, j: (i, 0, 0)),
                pl.BlockSpec((1, width, rank), lambda i, j: (i, 0, 0)),
                pl.BlockSpec((1, rank, width), lambda i, j: (j, 0, 0)),
                pl.BlockSpec((1, rank, width), lambda i, j: (j, 0, 0)),
                WHOLE],
            out_specs=pl.BlockSpec((1, 1, width, width), lambda i, j: (i, j, 0, 0)),
            compiler_params=params(),
        )(info, tile_ranks, tile_u, tile_v, uq1, uq2, vp1, vp2, cores)

    return on_device


def solution(mesh):
    placed = (P("row", "col", None, None), P("row", "col", None, None), P("row", "col"), P(), P())
    return jax.shard_map(
        make(mesh.shape["row"], mesh.shape["col"]),
        mesh=mesh,
        in_specs=placed,
        out_specs=P("row", "col", None, None),
        check_vma=False,
    )
```

time: 329 us -> 127 us (0.39)
  the two profiles are of different devices: /device:TPU:0 before, /device:TPU:13 now
where the time goes in v2:
time: 127 us; the launch traced here: 126 us
  waiting for transfers between devices  50.1 us (39%)
  starting transfers between devices  39.5 us (31%)
  Pallas kernels  16.6 us (13%)
  between operations  9.3 us (7%)
  local copies, waits for them, and re-layouts  6.02 us (5%)
  other arithmetic  4.2 us (3%)
    ppermute x25, waiting for transfers between devices, swap(): return lax.ppermute(block, axis, pairs)  50.1 us
    ppermute x25, starting transfers between devices, swap(): return lax.ppermute(block, axis, pairs)  39.5 us
    pallas_call x1, Pallas kernels, on_device(): pl.pallas_call(final_kernel, out_shape=jax.ShapeDtypeStruct((rows, cols,...  8.55 us
    pallas_call x1, Pallas kernels, on_device(): pl.pallas_call(solve_kernel, out_shape=jax.ShapeDtypeStruct((2, width, 3...  4.66 us
  transfers between devices with their start and end apart: 25, of which 10 were waited for; matrix products, arithmetic and copies ran while one was open for 5% of the time, Pallas kernels for 0%

profile of v2, /device:TPU:13, one launch (start us, length us, event | category | flops | bytes accessed | tf_op | source)
XLA Modules:
  0.0 125.8 jit_solution(10704119198701286841)
XLA Ops:
  0.0 1.5 %fusion.12 = (s32[1,1]{1,0:T(1,128)}, s32[1,1]{1,0:T(1,128)}, s32[1,1]{1,0:T(1,128)}, s32[1,1]{1,0:T(1,128)}) fusion(s32[2,2]{1,0:T(2,128)} %param.9), kind=kLoop, calls=%fused_computation.95 | loop fusion | bytes 32 | tf_op jit(solution)/shard_map/slice | solution.py:134
  7.2 2.4 %shard_map.55 = (bf16[1024,128]{1,0:T(8,128)(2,1)S(1)}, bf16[1024,128]{1,0:T(8,128)(2,1)}, bf16[1024,128]{1,0:T(8,128)(2,1)S(1)}, bf16[1024,128]{1,0:T(8,128)(2,...) custom-call(s32[4]{0:T(128)S(1)} %pad_add_fusion.info, ...), custom_call_target="tpu_custom_call" | custom-call | tf_op jit(solution)/shard_map/pallas_call | solution.py:144
  9.6 3.6 %collective-permute-start.5 = (bf16[128,1024]{1,0:T(8,128)(2,1)}, bf16[128,1024]{1,0:T(8,128)(2,1)}, u32[]{:S(2)}, u32[]{:S(2)}) collective-permute-start(bf16[128,1024]{1,0:T(8,128)(2,1)} %get-tuple-element.21), channel_id=1, source_target_pairs={{28,24},{0,0},{4,4},{8,8},{12,12},{16,16},{20,20},{29,25},{1,1},{5... | collective-permute-start | bytes 786440 | tf_op jit(solution)/shard_map/ppermute | solution.py:30
  14.4 3.6 %collective-permute-start.12 = (bf16[1024,128]{1,0:T(8,128)(2,1)}, bf16[1024,128]{1,0:T(8,128)(2,1)}, u32[]{:S(2)}, u32[]{:S(2)}) collective-permute-start(bf16[1024,128]{1,0:T(8,128)(2,1)} %get-tuple-element.25), channel_id=1, source_target_pairs={{28,24},{0,0},{4,4},{8,8},{12,12},{16,16},{20,20},{29,25},{1,1},{5... | collective-permute-start | bytes 786440 | tf_op jit(solution)/shard_map/ppermute | solution.py:30
  18.3 3.9 %collective-permute-start = (bf16[2,1024,128]{2,1,0:T(8,128)(2,1)S(1)}, bf16[2,1024,128]{2,1,0:T(8,128)(2,1)}, u32[]{:S(2)}, u32[]{:S(2)}) collective-permute-start(bf16[2,1024,128]{2,1,0:T(8,128)(2,1)S(1)} %get-tuple-element.17), channel_id=1, source_target_pairs={{3,2},{0,0},{1,1},{7,6},{4,4},{5,5},{11,10},{8,8},{9,9},{15,14},{1... | collective-permute-start | bytes 1572872 | tf_op jit(solution)/shard_map/ppermute | solution.py:30
  27.4 2.5 %stack.113.info = s32[6]{0:T(128)S(1)} concatenate(s32[1]{0:T(128)} %bitcast, s32[1]{0:T(128)} %bitcast.1, s32[1]{0:T(128)} %bitcast.2, s32[1]{0:T(128)} %bitcast.3, s32[1]{0:T(128)} %bitcast.4, s32[1]{0:T(128)} %bitcast.5), dimensions={0} | concatenate | bytes 48 | tf_op jit(solution)/shard_map/stack | solution.py:201
  30.0 1.3 %collective-permute-start.6 = (bf16[128,1024]{1,0:T(8,128)(2,1)S(1)}, bf16[128,1024]{1,0:T(8,128)(2,1)S(1)}, u32[]{:S(2)}, u32[]{:S(2)}) collective-permute-start(bf16[128,1024]{1,0:T(8,128)(2,1)S(1)} %broadcast_select_fusion.31), channel_id=1, source_target_pairs={{24,8},{28,12},{0,0},{4,4},{16,16},{20,20},{25,9},{29,13},{1,1},{5... | collective-permute-start | bytes 786440 | tf_op jit(solution)/shard_map/ppermute | solution.py:30
  32.4 1.3 %collective-permute-start.13 = (bf16[1024,128]{1,0:T(8,128)(2,1)S(1)}, bf16[1024,128]{1,0:T(8,128)(2,1)S(1)}, u32[]{:S(2)}, u32[]{:S(2)}) collective-permute-start(bf16[1024,128]{1,0:T(8,128)(2,1)S(1)} %broadcast_select_fusion.19), channel_id=1, source_target_pairs={{24,8},{28,12},{0,0},{4,4},{16,16},{20,20},{25,9},{29,13},{1,1},{5... | collective-permute-start | bytes 786440 | tf_op jit(solution)/shard_map/ppermute | solution.py:30
  34.7 6.1 %collective-permute-done.6 = bf16[128,1024]{1,0:T(8,128)(2,1)S(1)} collective-permute-done((bf16[128,1024]{1,0:T(8,128)(2,1)S(1)}, bf16[128,1024]{1,0:T(8,128)(2,1)S(1)}, u32[]{:S(2)}, u32[]{:S(2)}) %collective-permute-start.6) | collective-permute-done | bytes 262176 | tf_op jit(solution)/shard_map/ppermute | solution.py:30
  40.9 3.4 %collective-permute-start.7 = (bf16[128,1024]{1,0:T(8,128)(2,1)S(1)}, bf16[128,1024]{1,0:T(8,128)(2,1)S(1)}, u32[]{:S(2)}, u32[]{:S(2)}) collective-permute-start(bf16[128,1024]{1,0:T(8,128)(2,1)S(1)} %broadcast_select_fusion.32), channel_id=1, source_target_pairs={{8,0},{12,4},{24,16},{28,20},{9,1},{13,5},{25,17},{29,21},{10,2},{... | collective-permute-start | bytes 786440 | tf_op jit(solution)/shard_map/ppermute | solution.py:30
  44.3 7.8 %collective-permute-done.13 = bf16[1024,128]{1,0:T(8,128)(2,1)S(1)} collective-permute-done((bf16[1024,128]{1,0:T(8,128)(2,1)S(1)}, bf16[1024,128]{1,0:T(8,128)(2,1)S(1)}, u32[]{:S(2)}, u32[]{:S(2)}) %collective-permute-start.13) | collective-permute-done | bytes 262176 | tf_op jit(solution)/shard_map/ppermute | solution.py:30
  52.2 1.3 %collective-permute-start.14 = (bf16[1024,128]{1,0:T(8,128)(2,1)S(1)}, bf16[1024,128]{1,0:T(8,128)(2,1)S(1)}, u32[]{:S(2)}, u32[]{:S(2)}) collective-permute-start(bf16[1024,128]{1,0:T(8,128)(2,1)S(1)} %broadcast_select_fusion.20), channel_id=1, source_target_pairs={{8,0},{12,4},{24,16},{28,20},{9,1},{13,5},{25,17},{29,21},{10,2},{... | collective-permute-start | bytes 786440 | tf_op jit(solution)/shard_map/ppermute | solution.py:30
  53.5 7.7 %collective-permute-start.17 = (bf16[1024,128]{1,0:T(8,128)(2,1)S(1)}, bf16[1024,128]{1,0:T(8,128)(2,1)S(1)}, u32[]{:S(2)}, u32[]{:S(2)}) collective-permute-start(bf16[1024,128]{1,0:T(8,128)(2,1)S(1)} %broadcast_select_fusion.17), channel_id=1, source_target_pairs={{0,16},{4,20},{8,24},{12,28},{16,0},{20,4},{24,8},{28,12},{1,17},{... | collective-permute-start | bytes 786440 | tf_op jit(solution)/shard_map/ppermute | solution.py:30
  61.3 1.3 %collective-permute-start.1 = (bf16[2,1024,128]{2,1,0:T(8,128)(2,1)S(1)}, bf16[2,1024,128]{2,1,0:T(8,128)(2,1)S(1)}, u32[]{:S(2)}, u32[]{:S(2)}) collective-permute-start(bf16[2,1024,128]{2,1,0:T(8,128)(2,1)S(1)} %broadcast_select_fusion.4), channel_id=1, source_target_pairs={{2,0},{3,1},{6,4},{7,5},{10,8},{11,9},{14,12},{15,13},{18,16},{19,... | collective-permute-start | bytes 1572872 | tf_op jit(solution)/shard_map/ppermute | solution.py:30
  62.8 6.2 %collective-permute-done.10 = bf16[128,1024]{1,0:T(8,128)(2,1)S(1)} collective-permute-done((bf16[128,1024]{1,0:T(8,128)(2,1)S(1)}, bf16[128,1024]{1,0:T(8,128)(2,1)S(1)}, u32[]{:S(2)}, u32[]{:S(2)}) %collective-permute-start.10) | collective-permute-done | bytes 262176 | tf_op jit(solution)/shard_map/ppermute | solution.py:30
  69.8 10.5 %collective-permute-done.17 = bf16[1024,128]{1,0:T(8,128)(2,1)S(1)} collective-permute-done((bf16[1024,128]{1,0:T(8,128)(2,1)S(1)}, bf16[1024,128]{1,0:T(8,128)(2,1)S(1)}, u32[]{:S(2)}, u32[]{:S(2)}) %collective-permute-start.17) | collective-permute-done | bytes 262176 | tf_op jit(solution)/shard_map/ppermute | solution.py:30
  82.4 3.9 %collective-permute-start.22 = (bf16[2,64,1024]{2,1,0:T(8,128)(2,1)S(1)}, bf16[2,64,1024]{2,1,0:T(8,128)(2,1)S(1)}, u32[]{:S(2)}, u32[]{:S(2)}) collective-permute-start(bf16[2,64,1024]{2,1,0:T(8,128)(2,1)S(1)} %select_bitcast_fusion.2), channel_id=1, source_target_pairs={{0,1},{1,0},{2,3},{3,2},{4,5},{5,4},{6,7},{7,6},{8,9},{9,8},{10,11... | collective-permute-start | bytes 786440 | tf_op jit(solution)/shard_map/ppermute | solution.py:30
  86.3 6.5 %collective-permute-done.18 = bf16[2,1024,128]{2,1,0:T(8,128)(2,1)S(1)} collective-permute-done((bf16[2,1024,128]{2,1,0:T(8,128)(2,1)S(1)}, bf16[2,1024,128]{2,1,0:T(8,128)(2,1)S(1)}, u32[]{:S(2)}, u32[]{:S(2)}) %collective-permute-start.18) | collective-permute-done | bytes 524320 | tf_op jit(solution)/shard_map/ppermute | solution.py:30
  93.0 2.0 %collective-permute-start.19 = (bf16[2,512,128]{2,1,0:T(8,128)(2,1)S(1)}, bf16[2,512,128]{2,1,0:T(8,128)(2,1)S(1)}, u32[]{:S(2)}, u32[]{:S(2)}) collective-permute-start(bf16[2,512,128]{2,1,0:T(8,128)(2,1)S(1)} %select_bitcast_fusion.3), channel_id=1, source_target_pairs={{0,1},{1,0},{2,3},{3,2},{4,5},{5,4},{6,7},{7,6},{8,9},{9,8},{10,11... | collective-permute-start | bytes 786440 | tf_op jit(solution)/shard_map/ppermute | solution.py:30
  97.3 5.8 %collective-permute-done.23 = bf16[2,64,1024]{2,1,0:T(8,128)(2,1)S(1)} collective-permute-done((bf16[2,64,1024]{2,1,0:T(8,128)(2,1)S(1)}, bf16[2,64,1024]{2,1,0:T(8,128)(2,1)S(1)}, u32[]{:S(2)}, u32[]{:S(2)}) %collective-permute-start.23) | collective-permute-done | bytes 262176 | tf_op jit(solution)/shard_map/ppermute | solution.py:30
  103.2 1.3 %collective-permute-start.24 = (bf16[2,64,1024]{2,1,0:T(8,128)(2,1)S(1)}, bf16[2,64,1024]{2,1,0:T(8,128)(2,1)S(1)}, u32[]{:S(2)}, u32[]{:S(2)}) collective-permute-start(bf16[2,64,1024]{2,1,0:T(8,128)(2,1)S(1)} %broadcast_select_fusion.6), channel_id=1, source_target_pairs={{0,1},{1,0},{2,3},{3,2},{4,5},{5,4},{6,7},{7,6},{8,9},{9,8},{10,11... | collective-permute-start | bytes 786440 | tf_op jit(solution)/shard_map/ppermute | solution.py:30
  104.6 4.2 %collective-permute-done.20 = bf16[2,512,128]{2,1,0:T(8,128)(2,1)S(1)} collective-permute-done((bf16[2,512,128]{2,1,0:T(8,128)(2,1)S(1)}, bf16[2,512,128]{2,1,0:T(8,128)(2,1)S(1)}, u32[]{:S(2)}, u32[]{:S(2)}) %collective-permute-start.20) | collective-permute-done | bytes 262176 | tf_op jit(solution)/shard_map/ppermute | solution.py:30
  111.5 4.7 %shard_map.56.solved = bf16[2,1024,384]{2,1,0:T(8,128)(2,1)S(1)} custom-call(bf16[2,1024,1024]{2,1,0:T(8,128)(2,1)} %inverses.1, bf16[1024,128]{1,0:T(8,128)(2,1)S(1)} %get-tuple-element.72.refs_0_, bf16[1024,128]{1,0:T(8,128)(2,1)S(1)} %get-tuple-element.71.refs_1_, bf16[1024,128]{1,0:T(8,128)(2,1)S(1)} %get-tuple-element.67.refs_2_, ...), custom_call_target="tpu_custom_call" | custom-call | flops 1610612736 | bytes 6291456 | tf_op jit(solution)/shard_map/pallas_call | solution.py:185
  117.2 8.6 %shard_map.58 = bf16[2,2,1024,1024]{3,2,1,0:T(8,128)(2,1)} custom-call(s32[6]{0:T(128)S(1)} %stack.113.info, s32[2,2]{1,0:T(2,128)S(1)} %copy-done.4, bf16[2,2,1024,128]{3,2,1,0:T(8,128)(2,1)S(1)} %copy-done.1, bf16[2,2,128,1024]{3,2,1,0:T(8,128)(2,1)S(1)} %copy-done.2, bf16[2,1024,128]{2,1,0:T(8,128)(2,1)S(1)} %pad_maximum_fusion.1.uq1, ...), custom_call_target="tpu_custom_call" | custom-call | tf_op jit(solution)/shard_map/pallas_call | solution.py:202
  (80 shorter events, 15.1 us)
Async XLA Ops:
  9.6 20.3 %collective-permute-start.5 = (bf16[128,1024]{1,0:T(8,128)(2,1)}, bf16[128,1024]{1,0:T(8,128)(2,1)}, u32[]{:S(2)}, u32[]{:S(2)}) collective-permute-start(bf16[128,1024]{1,0:T(8,128)(2,1)} %get-tuple-element.21), channel_id=1, source_target_pairs={{28,24},{0,0},{4,4},{8,8},{12,12},{16,16},{20,20},{29,25},{1,1},{5... | collective-permute-start | bytes 786440 | tf_op jit(solution)/shard_map/ppermute | solution.py:30
  13.2 16.8 %collective-permute-start.8 = (bf16[128,1024]{1,0:T(8,128)(2,1)}, bf16[128,1024]{1,0:T(8,128)(2,1)}, u32[]{:S(2)}, u32[]{:S(2)}) collective-permute-start(bf16[128,1024]{1,0:T(8,128)(2,1)} %get-tuple-element.24), channel_id=1, source_target_pairs={{0,4},{4,0},{8,12},{12,8},{16,20},{20,16},{24,28},{28,24},{1,5},{5... | collective-permute-start | bytes 786440 | tf_op jit(solution)/shard_map/ppermute | solution.py:30
  14.4 17.9 %collective-permute-start.12 = (bf16[1024,128]{1,0:T(8,128)(2,1)}, bf16[1024,128]{1,0:T(8,128)(2,1)}, u32[]{:S(2)}, u32[]{:S(2)}) collective-permute-start(bf16[1024,128]{1,0:T(8,128)(2,1)} %get-tuple-element.25), channel_id=1, source_target_pairs={{28,24},{0,0},{4,4},{8,8},{12,12},{16,16},{20,20},{29,25},{1,1},{5... | collective-permute-start | bytes 786440 | tf_op jit(solution)/shard_map/ppermute | solution.py:30
  18.0 14.4 %collective-permute-start.15 = (bf16[1024,128]{1,0:T(8,128)(2,1)S(1)}, bf16[1024,128]{1,0:T(8,128)(2,1)}, u32[]{:S(2)}, u32[]{:S(2)}) collective-permute-start(bf16[1024,128]{1,0:T(8,128)(2,1)S(1)} %get-tuple-element.28), channel_id=1, source_target_pairs={{0,4},{4,0},{8,12},{12,8},{16,20},{20,16},{24,28},{28,24},{1,5},{5... | collective-permute-start | bytes 786440 | tf_op jit(solution)/shard_map/ppermute | solution.py:30
  18.3 35.3 %collective-permute-start = (bf16[2,1024,128]{2,1,0:T(8,128)(2,1)S(1)}, bf16[2,1024,128]{2,1,0:T(8,128)(2,1)}, u32[]{:S(2)}, u32[]{:S(2)}) collective-permute-start(bf16[2,1024,128]{2,1,0:T(8,128)(2,1)S(1)} %get-tuple-element.17), channel_id=1, source_target_pairs={{3,2},{0,0},{1,1},{7,6},{4,4},{5,5},{11,10},{8,8},{9,9},{15,14},{1... | collective-permute-start | bytes 1572872 | tf_op jit(solution)/shard_map/ppermute | solution.py:30
  29.9 31.4 %collective-permute-start.2 = (bf16[2,1024,128]{2,1,0:T(8,128)(2,1)S(1)}, bf16[2,1024,128]{2,1,0:T(8,128)(2,1)S(1)}, u32[]{:S(2)}, u32[]{:S(2)}) collective-permute-start(bf16[2,1024,128]{2,1,0:T(8,128)(2,1)S(1)} %get-tuple-element.20), channel_id=1, source_target_pairs={{0,1},{1,0},{2,3},{3,2},{4,5},{5,4},{6,7},{7,6},{8,9},{9,8},{10,11... | collective-permute-start | bytes 1572872 | tf_op jit(solution)/shard_map/ppermute | solution.py:30
  30.0 10.9 %collective-permute-start.6 = (bf16[128,1024]{1,0:T(8,128)(2,1)S(1)}, bf16[128,1024]{1,0:T(8,128)(2,1)S(1)}, u32[]{:S(2)}, u32[]{:S(2)}) collective-permute-start(bf16[128,1024]{1,0:T(8,128)(2,1)S(1)} %broadcast_select_fusion.31), channel_id=1, source_target_pairs={{24,8},{28,12},{0,0},{4,4},{16,16},{20,20},{25,9},{29,13},{1,1},{5... | collective-permute-start | bytes 786440 | tf_op jit(solution)/shard_map/ppermute | solution.py:30
  32.3 8.6 %collective-permute-start.9 = (bf16[128,1024]{1,0:T(8,128)(2,1)S(1)}, bf16[128,1024]{1,0:T(8,128)(2,1)S(1)}, u32[]{:S(2)}, u32[]{:S(2)}) collective-permute-start(bf16[128,1024]{1,0:T(8,128)(2,1)S(1)} %broadcast_select_fusion.28), channel_id=1, source_target_pairs={{0,8},{4,12},{8,0},{12,4},{16,24},{20,28},{24,16},{28,20},{1,9},{5... | collective-permute-start | bytes 786440 | tf_op jit(solution)/shard_map/ppermute | solution.py:30
  32.4 19.7 %collective-permute-start.13 = (bf16[1024,128]{1,0:T(8,128)(2,1)S(1)}, bf16[1024,128]{1,0:T(8,128)(2,1)S(1)}, u32[]{:S(2)}, u32[]{:S(2)}) collective-permute-start(bf16[1024,128]{1,0:T(8,128)(2,1)S(1)} %broadcast_select_fusion.19), channel_id=1, source_target_pairs={{24,8},{28,12},{0,0},{4,4},{16,16},{20,20},{25,9},{29,13},{1,1},{5... | collective-permute-start | bytes 786440 | tf_op jit(solution)/shard_map/ppermute | solution.py:30
  40.9 11.3 %collective-permute-start.16 = (bf16[1024,128]{1,0:T(8,128)(2,1)S(1)}, bf16[1024,128]{1,0:T(8,128)(2,1)S(1)}, u32[]{:S(2)}, u32[]{:S(2)}) collective-permute-start(bf16[1024,128]{1,0:T(8,128)(2,1)S(1)} %broadcast_select_fusion.16), channel_id=1, source_target_pairs={{0,8},{4,12},{8,0},{12,4},{16,24},{20,28},{24,16},{28,20},{1,9},{5... | collective-permute-start | bytes 786440 | tf_op jit(solution)/shard_map/ppermute | solution.py:30
  40.9 21.8 %collective-permute-start.7 = (bf16[128,1024]{1,0:T(8,128)(2,1)S(1)}, bf16[128,1024]{1,0:T(8,128)(2,1)S(1)}, u32[]{:S(2)}, u32[]{:S(2)}) collective-permute-start(bf16[128,1024]{1,0:T(8,128)(2,1)S(1)} %broadcast_select_fusion.32), channel_id=1, source_target_pairs={{8,0},{12,4},{24,16},{28,20},{9,1},{13,5},{25,17},{29,21},{10,2},{... | collective-permute-start | bytes 786440 | tf_op jit(solution)/shard_map/ppermute | solution.py:30
  52.1 16.9 %collective-permute-start.10 = (bf16[128,1024]{1,0:T(8,128)(2,1)S(1)}, bf16[128,1024]{1,0:T(8,128)(2,1)S(1)}, u32[]{:S(2)}, u32[]{:S(2)}) collective-permute-start(bf16[128,1024]{1,0:T(8,128)(2,1)S(1)} %broadcast_select_fusion.29), channel_id=1, source_target_pairs={{0,16},{4,20},{8,24},{12,28},{16,0},{20,4},{24,8},{28,12},{1,17},{... | collective-permute-start | bytes 786440 | tf_op jit(solution)/shard_map/ppermute | solution.py:30
  52.2 17.6 %collective-permute-start.14 = (bf16[1024,128]{1,0:T(8,128)(2,1)S(1)}, bf16[1024,128]{1,0:T(8,128)(2,1)S(1)}, u32[]{:S(2)}, u32[]{:S(2)}) collective-permute-start(bf16[1024,128]{1,0:T(8,128)(2,1)S(1)} %broadcast_select_fusion.20), channel_id=1, source_target_pairs={{8,0},{12,4},{24,16},{28,20},{9,1},{13,5},{25,17},{29,21},{10,2},{... | collective-permute-start | bytes 786440 | tf_op jit(solution)/shard_map/ppermute | solution.py:30
  53.5 26.7 %collective-permute-start.17 = (bf16[1024,128]{1,0:T(8,128)(2,1)S(1)}, bf16[1024,128]{1,0:T(8,128)(2,1)S(1)}, u32[]{:S(2)}, u32[]{:S(2)}) collective-permute-start(bf16[1024,128]{1,0:T(8,128)(2,1)S(1)} %broadcast_select_fusion.17), channel_id=1, source_target_pairs={{0,16},{4,20},{8,24},{12,28},{16,0},{20,4},{24,8},{28,12},{1,17},{... | collective-permute-start | bytes 786440 | tf_op jit(solution)/shard_map/ppermute | solution.py:30
  61.3 19.7 %collective-permute-start.1 = (bf16[2,1024,128]{2,1,0:T(8,128)(2,1)S(1)}, bf16[2,1024,128]{2,1,0:T(8,128)(2,1)S(1)}, u32[]{:S(2)}, u32[]{:S(2)}) collective-permute-start(bf16[2,1024,128]{2,1,0:T(8,128)(2,1)S(1)} %broadcast_select_fusion.4), channel_id=1, source_target_pairs={{2,0},{3,1},{6,4},{7,5},{10,8},{11,9},{14,12},{15,13},{18,16},{19,... | collective-permute-start | bytes 1572872 | tf_op jit(solution)/shard_map/ppermute | solution.py:30
  62.7 19.4 %collective-permute-start.3 = (bf16[2,1024,128]{2,1,0:T(8,128)(2,1)S(1)}, bf16[2,1024,128]{2,1,0:T(8,128)(2,1)S(1)}, u32[]{:S(2)}, u32[]{:S(2)}) collective-permute-start(bf16[2,1024,128]{2,1,0:T(8,128)(2,1)S(1)} %broadcast_select_fusion.2), channel_id=1, source_target_pairs={{0,2},{1,3},{2,0},{3,1},{4,6},{5,7},{6,4},{7,5},{8,10},{9,11},{10,... | collective-permute-start | bytes 1572872 | tf_op jit(solution)/shard_map/ppermute | solution.py:30
  69.2 13.1 %collective-permute-start.11 = (bf16[2,128,1024]{2,1,0:T(8,128)(2,1)S(1)}, bf16[2,128,1024]{2,1,0:T(8,128)(2,1)S(1)}, u32[]{:S(2)}, u32[]{:S(2)}) collective-permute-start(bf16[2,128,1024]{2,1,0:T(8,128)(2,1)S(1)} %pad_maximum_fusion.3), channel_id=1, source_target_pairs={{0,4},{4,0},{8,12},{12,8},{16,20},{20,16},{24,28},{28,24},{1,5},{5... | collective-permute-start | bytes 1572872 | tf_op jit(solution)/shard_map/ppermute | solution.py:30
  80.4 12.5 %collective-permute-start.18 = (bf16[2,1024,128]{2,1,0:T(8,128)(2,1)S(1)}, bf16[2,1024,128]{2,1,0:T(8,128)(2,1)S(1)}, u32[]{:S(2)}, u32[]{:S(2)}) collective-permute-start(bf16[2,1024,128]{2,1,0:T(8,128)(2,1)S(1)} %pad_maximum_fusion.6), channel_id=1, source_target_pairs={{0,4},{4,0},{8,12},{12,8},{16,20},{20,16},{24,28},{28,24},{1,5},{5... | collective-permute-start | bytes 1572872 | tf_op jit(solution)/shard_map/ppermute | solution.py:30
  82.4 12.6 %collective-permute-start.22 = (bf16[2,64,1024]{2,1,0:T(8,128)(2,1)S(1)}, bf16[2,64,1024]{2,1,0:T(8,128)(2,1)S(1)}, u32[]{:S(2)}, u32[]{:S(2)}) collective-permute-start(bf16[2,64,1024]{2,1,0:T(8,128)(2,1)S(1)} %select_bitcast_fusion.2), channel_id=1, source_target_pairs={{0,1},{1,0},{2,3},{3,2},{4,5},{5,4},{6,7},{7,6},{8,9},{9,8},{10,11... | collective-permute-start | bytes 786440 | tf_op jit(solution)/shard_map/ppermute | solution.py:30
  93.0 3.2 %collective-permute-start.19 = (bf16[2,512,128]{2,1,0:T(8,128)(2,1)S(1)}, bf16[2,512,128]{2,1,0:T(8,128)(2,1)S(1)}, u32[]{:S(2)}, u32[]{:S(2)}) collective-permute-start(bf16[2,512,128]{2,1,0:T(8,128)(2,1)S(1)} %select_bitcast_fusion.3), channel_id=1, source_target_pairs={{0,1},{1,0},{2,3},{3,2},{4,5},{5,4},{6,7},{7,6},{8,9},{9,8},{10,11... | collective-permute-start | bytes 786440 | tf_op jit(solution)/shard_map/ppermute | solution.py:30
  95.1 8.0 %collective-permute-start.23 = (bf16[2,64,1024]{2,1,0:T(8,128)(2,1)S(1)}, bf16[2,64,1024]{2,1,0:T(8,128)(2,1)S(1)}, u32[]{:S(2)}, u32[]{:S(2)}) collective-permute-start(bf16[2,64,1024]{2,1,0:T(8,128)(2,1)S(1)} %bitcast_select_fusion), channel_id=1, source_target_pairs={{0,2},{1,3},{2,0},{3,1},{4,6},{5,7},{6,4},{7,5},{8,10},{9,11},{10,... | collective-permute-start | bytes 786440 | tf_op jit(solution)/shard_map/ppermute | solution.py:30
  95.3 15.6 %collective-permute-start.4 = (bf16[2,2,1024,128]{3,2,1,0:T(8,128)(2,1)S(1)}, bf16[2,2,1024,128]{3,2,1,0:T(8,128)(2,1)S(1)}, u32[]{:S(2)}, u32[]{:S(2)}) collective-permute-start(bf16[2,2,1024,128]{3,2,1,0:T(8,128)(2,1)S(1)} %pad_maximum_fusion), channel_id=1, source_target_pairs={{0,1},{1,0},{2,3},{3,2},{4,5},{5,4},{6,7},{7,6},{8,9},{9,8},{10,11... | collective-permute-start | bytes 3145736 | tf_op jit(solution)/shard_map/ppermute | solution.py:30
  96.3 12.4 %collective-permute-start.20 = (bf16[2,512,128]{2,1,0:T(8,128)(2,1)S(1)}, bf16[2,512,128]{2,1,0:T(8,128)(2,1)S(1)}, u32[]{:S(2)}, u32[]{:S(2)}) collective-permute-start(bf16[2,512,128]{2,1,0:T(8,128)(2,1)S(1)} %bitcast_select_fusion.1), channel_id=1, source_target_pairs={{0,2},{1,3},{2,0},{3,1},{4,6},{5,7},{6,4},{7,5},{8,10},{9,11},{10,... | collective-permute-start | bytes 786440 | tf_op jit(solution)/shard_map/ppermute | solution.py:30
  103.2 6.5 %collective-permute-start.24 = (bf16[2,64,1024]{2,1,0:T(8,128)(2,1)S(1)}, bf16[2,64,1024]{2,1,0:T(8,128)(2,1)S(1)}, u32[]{:S(2)}, u32[]{:S(2)}) collective-permute-start(bf16[2,64,1024]{2,1,0:T(8,128)(2,1)S(1)} %broadcast_select_fusion.6), channel_id=1, source_target_pairs={{0,1},{1,0},{2,3},{3,2},{4,5},{5,4},{6,7},{7,6},{8,9},{9,8},{10,11... | collective-permute-start | bytes 786440 | tf_op jit(solution)/shard_map/ppermute | solution.py:30
  (6 other events, 21.0 us)
